TPU v7x, 256 devices: a whole 4x4x8 slice. The times are simulated.
256 devices in a mesh: dp: 32 (over z, y), tensor: 8 (over x, core).
Axes of the slice: x: 4, y: 4, z: 8, core: 2. Of those that a mesh axis runs over, the one named last changes fastest.
Arguments:
- hidden: bfloat16 [128, 256, 4096], P('dp'), may hold values from -6 to 6
- lengths: int32 [128], P('dp'), may hold values from 1 to 256, 19660 in all
- judge: bfloat16 [512, 16, 4096], P('dp', None, 'tensor'), may hold values from -6 to 6
- w_query: bfloat16 [4096, 4096], P(None, 'tensor'), may hold values from -0.09375 to 0.09375
- w_keyval: bfloat16 [4096, 2048], P(None, 'tensor'), may hold values from -0.09375 to 0.09375
- pair_devices: int32 [512, 2], P('dp'), may hold values from 0 to 31, as said below
- pair_items: int32 [512, 2], P('dp'), may hold values from 0 to 3, as said below
Outputs:
- encoded: bfloat16 [128, 256, 4096], P('dp', None, 'tensor')
- pair_attended: bfloat16 [512, 16, 4096], P('dp', None, 'tensor')
Inputs may be any that keep to these rules, and one draw needn't show every extreme that they name: `pair_devices`: each prompt's responses are spread over a band of 8 consecutive dp indices, so that their ragged lengths share the load: index 8 b + k holds at place i the k-th response of band b's prompt i. The two sides of a pair are two responses of one prompt (same band, same place, different indices). In each aligned block of 16 rows (the pairs of one dp index) no index is named more than 2 times, and some index exactly 2 times. `pair_items`: both sides of a pair have the same place.
All inputs are finite; a program needn't handle non-finite values. No bound on the sum of `lengths` on one device may be relied on, other than what follows from the above.
Results may differ from a plain program's by a relative error of at most 0.0069.
Values may be sent and summed in bfloat16 or wider, within the bound.
A program may use at most 128 MiB of HBM per device.

v0:
```python
import jax
import jax.numpy as jnp
from jax import lax
from jax.sharding import PartitionSpec as P

HD = 128


softcap_limit = 5.0


def capped(scores):
    return softcap_limit * jnp.tanh(scores / softcap_limit)


def on_device(hidden, lengths, judge, w_query, w_keyval, pair_devices, pair_items):
    ndevices = lax.axis_size("dp")
    resp_local, seq, width = hidden.shape
    head_cols = w_query.shape[1]
    heads_here = head_cols // HD
    kv_here = w_keyval.shape[1] // (2 * HD)
    group = heads_here // kv_here
    pairs_here = judge.shape[0]
    query_len = judge.shape[1]
    slots = max(2, 2 * pairs_here // ndevices)
    scale = HD ** (-0.5)
    positions = jnp.arange(seq, dtype=jnp.int32)
    flat = hidden.reshape(resp_local * seq, width)
    queries = jnp.dot(flat, w_query, preferred_element_type=jnp.float32).astype(jnp.bfloat16)
    queries = queries.reshape(resp_local, seq, kv_here, group, HD)
    keyval = jnp.dot(flat, w_keyval, preferred_element_type=jnp.float32).astype(jnp.bfloat16)
    keyval = keyval.reshape(resp_local, seq, kv_here, 2, HD)
    scores = capped(
        jnp.einsum(
            "rqkgd,rtkd->rkgqt", queries, keyval[:, :, :, 0], preferred_element_type=jnp.float32
        )
        * scale
    )
    causal = positions[None, :] <= positions[:, None]
    allowed = causal[None] & (positions[None, None, :] < lengths[:, None, None])
    weights = jnp.where(allowed[:, None, None], jnp.exp(scores), 0.0)
    probs = (weights / jnp.sum(weights, -1, keepdims=True)).astype(jnp.bfloat16)
    encoded = jnp.einsum(
        "rkgqt,rtkd->rqkgd", probs, keyval[:, :, :, 1], preferred_element_type=jnp.float32
    )
    encoded = encoded.reshape(resp_local, seq, head_cols).astype(jnp.bfloat16)
    judge_rows = judge.reshape(pairs_here * query_len, judge.shape[2])
    judge_q = jnp.dot(
        lax.all_gather(judge_rows, "tensor", axis=1, tiled=True),
        w_query,
        preferred_element_type=jnp.float32,
    ).astype(jnp.bfloat16)
    sides = pairs_here * 2
    targets = pair_devices.reshape(sides)
    items = pair_items.reshape(sides)
    onehot = (targets[:, None] == jnp.arange(ndevices, dtype=jnp.int32)[None, :]).astype(jnp.int32)
    earlier = jnp.cumsum(onehot, 0) - onehot
    place = targets * slots + jnp.sum(earlier * onehot, 1)
    request = (
        jnp.full((ndevices * slots,), -1, jnp.int32).at[place].set(items).reshape(ndevices, slots)
    )
    wanted = lax.all_to_all(request, "dp", split_axis=0, concat_axis=0, tiled=True)
    picked = jnp.maximum(wanted, 0).reshape(ndevices * slots)
    every_length = lax.all_gather(lengths, "dp", axis=0, tiled=True)
    outgoing = jnp.take(keyval.reshape(resp_local, seq, kv_here * 2 * HD), picked, axis=0)
    outgoing = outgoing.reshape(ndevices, slots, seq, kv_here * 2 * HD)
    arrived = lax.all_to_all(outgoing, "dp", split_axis=0, concat_axis=0, tiled=True)
    arrived = arrived.reshape(ndevices * slots, seq, kv_here, 2, HD)
    side_kv = jnp.take(arrived, place, axis=0).reshape(pairs_here, 2, seq, kv_here, 2, HD)
    side_len = jnp.take(every_length, targets * resp_local + items).reshape(pairs_here, 2)
    judge_heads = judge_q.reshape(pairs_here, query_len, kv_here, group, HD)
    pair_scores = capped(
        jnp.einsum(
            "pmkgd,pstkd->pkgmst",
            judge_heads,
            side_kv[:, :, :, :, 0],
            preferred_element_type=jnp.float32,
        )
        * scale
    )
    live = positions[None, None, :] < side_len[:, :, None]
    pair_weights = jnp.where(live[:, None, None, None], jnp.exp(pair_scores), 0.0)
    totals = jnp.sum(pair_weights, (4, 5))
    summed = jnp.einsum(
        "pkgmst,pstkd->pmkgd",
        pair_weights.astype(jnp.bfloat16),
        side_kv[:, :, :, :, 1],
        preferred_element_type=jnp.float32,
    )
    attended = summed / jnp.transpose(totals, (0, 3, 1, 2))[..., None]
    pair_attended = attended.reshape(pairs_here, query_len, head_cols).astype(jnp.bfloat16)
    return (encoded, pair_attended)


def solution(mesh):
    return jax.shard_map(
        on_device,
        mesh=mesh,
        in_specs=(
            P("dp", None, None),
            P("dp"),
            P("dp", None, "tensor"),
            P(None, "tensor"),
            P(None, "tensor"),
            P("dp", None),
            P("dp", None),
        ),
        out_specs=(P("dp", None, "tensor"), P("dp", None, "tensor")),
        check_vma=False,
    )
```

profile of v0, /device:TPU:28, one launch (start us, length us, event | category | flops | bytes accessed | tf_op | source)
XLA Modules:
  0.0 314.7 jit_solution(16719310670414796834)
XLA Ops:
  7.2 0.9 copy.84
  8.1 0.7 multiply_add_fusion
  8.8 0.8 copy.88
  9.5 0.1 reshape.267
  9.8 0.2 select_reduce_fusion
  9.9 0.1 copy.87
  10.0 0.1 mul.63
  10.1 0.1 reshape.307
  10.2 0.7 scatter_custom_fusion
  10.9 0.7 all_to_all.9
  11.6 11.5 %all-to-all-start = ((s32[32,1,2]{2,1,0:T(1,128)}), s32[32,1,2]{2,1,0:T(1,128)S(1)}, u32[]{:S(2)}, u32[]{:S(2)}) async-start(s32[32,1,2]{2,1,0:T(1,128)} %bitcast.4), calls=%async_computation | async-start | bytes 32768 | tf_op jit(solution)/shard_map/all_to_all | solution.py:62
  23.1 5.7 %convolution_convert_fusion.1 = bf16[1024,256]{1,0:T(8,128)(2,1)S(1)} fusion(bf16[1024,4096]{1,0:T(8,128)(2,1)} %bitcast.127, bf16[4096,256]{1,0:T(8,128)(2,1)S(1)} %copy-done), kind=kOutput, calls=%fused_computation.21 | convolution fusion | flops 2147745792 | bytes 11010048 | tf_op jit(solution)/shard_map/dot_general | solution.py:31
  28.8 2.2 all-to-all-done
  31.0 0.1 reshape.279
  31.2 5.4 %gather_fusion = bf16[64,256,256]{2,1,0:T(8,128)(2,1)} fusion(bf16[4,256,256]{2,1,0:T(8,128)(2,1)S(1)} %bitcast.120, s32[1024]{0:T(1024)S(1)} %pad_clamp_fusion.2), kind=kCustom, calls=%fused_computation | custom fusion | bytes 16777472 | tf_op jit(solution)/shard_map/jit(_take)/gather | solution.py:65
  36.5 11.9 %copy.92 = bf16[64,256,256]{1,2,0:T(8,128)(2,1)} copy(bf16[64,256,256]{2,1,0:T(8,128)(2,1)} %gather_fusion) | data formatting | bytes 16777216 | tf_op jit(solution)/shard_map/jit(_take)/gather | solution.py:65
  48.5 0.1 copy.90
  48.6 0.1 copy.91
  48.7 7.5 %broadcast_select_fusion = bf16[32,2,256,256]{2,3,1,0:T(8,128)(2,1)} fusion(bf16[32,2,256,256]{2,3,1,0:T(8,128)(2,1)} %bitcast.121, pred[32,2]{1,0:T(8,128)(4,1)S(1)} %copy.91), kind=kLoop, calls=%fused_computation.4 | loop fusion | flops 4194304 | bytes 16777280 | tf_op jit(solution)/shard_map/jit(_take)/select_n | solution.py:65
  56.2 7.9 %all-to-all-start.1 = ((bf16[32,2,256,256]{2,3,1,0:T(8,128)(2,1)}), bf16[32,2,256,256]{2,3,1,0:T(8,128)(2,1)}, u32[]{:S(2)}, u32[]{:S(2)}) async-start(bf16[32,2,256,256]{2,3,1,0:T(8,128)(2,1)} %broadcast_select_fusion), calls=%async_computation.1 | async-start | bytes 16777216 | tf_op jit(solution)/shard_map/all_to_all | solution.py:67
  64.1 0.7 all-gather.2.cloned.1.call-update
  64.8 0.1 reshape.262
  65.1 0.1 copy.86
  65.3 0.1 add.95
  65.4 0.6 dynamic-slice
  66.6 0.2 dynamic-update-slice
  66.9 194.7 %all-reduce = s32[128]{0:T(128)S(1)} all-reduce(s32[128]{0:T(128)S(1)} %dynamic-update-slice), channel_id=1, replica_groups=mesh['dp'=32,'tensor'=8] {'dp'}, use_global_device_ids=true, to_apply=%add | all-reduce | flops 128 | bytes 1024
  261.6 0.7 gather_fusion.2
  262.4 0.1 copy.96
  262.5 0.1 copy.97
  262.6 10.0 %convolution_convert_fusion = bf16[1024,512]{1,0:T(8,128)(2,1)} fusion(bf16[1024,4096]{1,0:T(8,128)(2,1)} %bitcast.128, bf16[4096,512]{1,0:T(8,128)(2,1)} %param.10), kind=kOutput, calls=%fused_computation.19 | convolution fusion | flops 4295491584 | bytes 13631488 | tf_op jit(solution)/shard_map/dot_general | solution.py:29
  272.6 1.3 reshape.265
  274.0 0.7 fusion.26
  274.7 0.4 copy.111
  275.2 0.2 broadcast_and_fusion
  275.4 1.7 fusion
  277.1 1.5 fusion.6
  278.6 1.3 copy.101
  279.9 0.1 iota_compare_fusion.1
  280.0 4.1 %convolution_convert_fusion.2 = bf16[256,512]{1,0:T(8,128)(2,1)S(1)} fusion(bf16[256,4096]{1,0:T(8,128)(2,1)} %all-gather.2.cloned.1.call-done, bf16[4096,512]{1,0:T(8,128)(2,1)} %param.10), kind=kOutput, calls=%fused_computation.23 | convolution fusion | flops 1073872896 | bytes 6553600 | tf_op jit(solution)/shard_map/dot_general | solution.py:48
  284.2 11.9 %copy.93 = bf16[64,256,2,128]{3,1,2,0:T(8,128)(2,1)} copy(bf16[64,256,2,128]{1,3,2,0:T(8,128)(2,1)} %bitcast.9) | data formatting | bytes 16777216 | tf_op jit(solution)/shard_map/reshape | solution.py:68
  296.1 6.4 %gather_fusion.1 = bf16[32,256,2,128]{3,1,2,0:T(8,128)(2,1)} fusion(bf16[64,256,2,128]{3,1,2,0:T(8,128)(2,1)} %copy.93, s32[1024]{0:T(1024)S(1)} %pad_clamp_fusion.1), kind=kCustom, calls=%fused_computation.1 | custom fusion | bytes 8388736 | tf_op jit(solution)/shard_map/jit(_take)/gather | solution.py:69
  302.5 2.5 copy.94
  304.9 0.5 broadcast_select_fusion.1
  305.4 1.0 bitcast_reduce_fusion
  306.4 0.5 fusion.11
  307.0 0.1 copy.100
  307.1 0.8 convert_element_type.47
  (32 shorter events, 0.8 us)
Async XLA Ops:
  7.2 15.9 %copy-start = (bf16[4096,256]{1,0:T(8,128)(2,1)S(1)}, bf16[4096,256]{1,0:T(8,128)(2,1)}, u32[]{:S(2)}) copy-start(bf16[4096,256]{1,0:T(8,128)(2,1)} %param.11) | copy-start | bytes 6291460
  11.6 19.4 %all-to-all-start = ((s32[32,1,2]{2,1,0:T(1,128)}), s32[32,1,2]{2,1,0:T(1,128)S(1)}, u32[]{:S(2)}, u32[]{:S(2)}) async-start(s32[32,1,2]{2,1,0:T(1,128)} %bitcast.4), calls=%async_computation | async-start | bytes 32768 | tf_op jit(solution)/shard_map/all_to_all | solution.py:62
  56.2 8.9 %copy-start.2 = (s32[16,2]{0,1:T(2,128)S(1)}, s32[16,2]{0,1:T(2,128)}, u32[]{:S(2)}) copy-start(s32[16,2]{0,1:T(2,128)} %param.12) | copy-start | bytes 388
  56.2 9.2 %copy-start.4 = (u32[256]{0:T(256)S(1)}, u32[256]{0:T(256)}, u32[]{:S(2)}) copy-start(u32[256]{0:T(256)} %constant.80) | copy-start | bytes 3076
  56.2 10.5 %copy-start.3 = (s32[4]{0:T(128)S(1)}, s32[4]{0:T(128)}, u32[]{:S(2)}) copy-start(s32[4]{0:T(128)} %param.8) | copy-start | bytes 52
  56.2 228.0 %all-to-all-start.1 = ((bf16[32,2,256,256]{2,3,1,0:T(8,128)(2,1)}), bf16[32,2,256,256]{2,3,1,0:T(8,128)(2,1)}, u32[]{:S(2)}, u32[]{:S(2)}) async-start(bf16[32,2,256,256]{2,3,1,0:T(8,128)(2,1)} %broadcast_select_fusion), calls=%async_computation.1 | async-start | bytes 16777216 | tf_op jit(solution)/shard_map/all_to_all | solution.py:67
  64.0 216.0 %all-gather.2.cloned.1.call-start = ((), (), s32[]{:S(2)}) async-start(), calls=%async_computation.2 | async-start | bytes 2359296 | tf_op jit(solution)/shard_map/all_gather | solution.py:49
  305.4 2.5 copy-start.1
Sparse Core Ops, SparseCore 0:
  66.7 27.6 all-gather.1
where the time goes:
time: 316 us; the launch traced here: 315 us
  blocking collectives  195 us (62%)
  local copies, waits for them, and re-layouts  48.8 us (15%)
  matrix products  24.5 us (8%)
  starting transfers between devices  19.4 us (6%)
  between operations  14.9 us (5%)
  other arithmetic  9.48 us (3%)
    unnamed x1, blocking collectives  195 us
    gather x2, local copies, waits for them, and re-layouts, on_device(): jnp.take(keyval.reshape(resp_local, seq, kv_here * 2 * HD), picked, axis=0)  17.3 us
    reshape x1, local copies, waits for them, and re-layouts, on_device(): arrived = arrived.reshape(ndevices * slots, seq, kv_here, 2, HD)  11.9 us
    all_to_all x1, starting transfers between devices, on_device(): lax.all_to_all(request, 'dp', split_axis=0, concat_axis=0, tiled=True)  11.5 us
    dot_general x1, matrix products, on_device(): jnp.dot(flat, w_query, preferred_element_type=jnp.float32)  10 us
    gather x2, local copies, waits for them, and re-layouts, on_device(): jnp.take(arrived, place, axis=0).reshape(pairs_here, 2, seq, kv_here, 2, HD)  8.85 us
    all_to_all x1, starting transfers between devices, on_device(): lax.all_to_all(outgoing, 'dp', split_axis=0, concat_axis=0, tiled=True)  7.86 us
    select_n x1, other arithmetic, on_device(): jnp.take(keyval.reshape(resp_local, seq, kv_here * 2 * HD), picked, axis=0)  7.46 us
  transfers between devices with their start and end apart: 3, of which 1 were waited for; matrix products, arithmetic and copies ran while one was open for 9% of the time, Pallas kernels for 0%

commit v1 on v0

v1 whole, which is shorter than its diff:
```python
import functools
import math
import jax
import jax.numpy as jnp
from jax import lax
from jax.experimental import pallas as pl
from jax.experimental.pallas import tpu as pltpu
from jax.sharding import PartitionSpec as P

HD = 128
C = 4
BF = jnp.bfloat16
F32 = jnp.float32
I32 = jnp.int32
MESH = pl.DeviceIdType.MESH
CAP_IN = HD ** -0.5 / 5.0
CAP_OUT = 5.0 * math.log2(math.e)

SCHED = (
    "KV0", "KV1", "KV2", "KV3", "XF0", "MY", "Q0", "MR", "Z0", "QP0",
    "XF1", "Y00", "Q1", "Z1", "QP1", "ML", "Y10", "XF2", "Q2", "MW",
    "Z2", "QP2", "Y20", "XF3", "Q3", "Z3", "QP3", "Y30", "VP", "A00",
    "Y03", "Y02", "Y01", "A10", "R00", "A20", "Y13", "Y12", "Y11", "A30",
    "A03", "Y23", "Y22", "Y21", "A02", "R10", "R20", "Y33", "A01", "Y32",
    "Y31", "A13", "R30", "A12", "R03", "A11", "SA0", "A23", "A22", "R02",
    "A21", "R01", "A33", "A32", "R13", "R12", "A31", "SA1", "R11", "R23",
    "R22", "SA2", "R21", "R33", "R32", "SA3", "R31", "H",
)


def weights_of(scores):
    return jnp.exp2(jnp.tanh(scores * CAP_IN) * CAP_OUT)


def kernel(judge, hidden, wq, wkv, lens, pdev, pitem, enc, pair, *scratch):
    (hid_v, wq_v, wkv_v, jin, jb, qself, kvx, vext, zs, ys, yq, rs, zr, mt, sm, smr, sm0, lt, ls,
     oenc, opair, lsem, ssem, rsem, qb, zq, yr, hret) = scratch
    npair, ntok, kslice = judge.shape
    tc = ntok // C
    rows = tc * 4
    per = rows // 16
    dp = lax.axis_index("dp")
    t = lax.axis_index("tensor")
    z, y = dp // 4, lax.rem(dp, 4)
    x, core = t // 2, lax.rem(t, 2)
    odd = lax.rem(z, 2)
    sg = 2 * odd - 1
    band = z // 2

    def mod(a, n):
        return lax.rem(a + 4 * n, n)

    zt = [z, mod(z + sg, 8), mod(z - 2 * sg, 8), mod(z + 3 * sg, 8)]
    zh = [z] + [mod(z + n * sg, 8) for n in (1, 2, 3)]

    def at(zz=None, yy=None, xx=None, cc=None):
        zz, yy = (z if zz is None else zz), (y if yy is None else yy)
        xx, cc = (x if xx is None else xx), (core if cc is None else cc)
        return (zz * 4 + yy, xx * 2 + cc)

    local_count = [0]
    recv_of, send_of, finals = {}, {}, []

    def remote(name, src, dst, dev, group, total):
        if group not in send_of:
            send_of[group] = len(send_of)
            finals.append((send_of[group], total))
        if name not in recv_of:
            recv_of[name] = len(recv_of)
        pltpu.make_async_remote_copy(
            src_ref=src, dst_ref=dst, send_sem=ssem.at[send_of[group]], recv_sem=rsem.at[recv_of[name]],
            device_id=dev, device_id_type=MESH).start()

    def arrived(name, dst):
        if name not in recv_of:
            recv_of[name] = len(recv_of)
        pltpu.make_async_remote_copy(
            src_ref=dst, dst_ref=dst, send_sem=ssem.at[0], recv_sem=rsem.at[recv_of[name]],
            device_id=(dp, t), device_id_type=MESH).wait_recv()

    def local(src, dst):
        copy = pltpu.make_async_copy(src, dst, lsem.at[local_count[0]])
        local_count[0] += 1
        copy.start()
        return copy

    l_j = local(judge, jin)
    l_kv = local(wkv, wkv_v)
    l_h = [local(hidden.at[0], hid_v.at[0]), local(hidden.at[1], hid_v.at[1])]
    l_q = local(wq, wq_v)
    l_h += [local(hidden.at[2], hid_v.at[2]), local(hidden.at[3], hid_v.at[3])]

    barrier = pltpu.get_barrier_semaphore()
    peers = [at(xx=mod(x + d, 4)) for d in (1, 2, 3)] + [at(cc=1 - core)]
    peers += [at(yy=mod(y + d, 4)) for d in (1, 2, 3)]
    peers += [at(zz=mod(z + d, 8)) for d in (1, -1, 2, -2, 3, -3)]
    for dev in peers:
        pl.semaphore_signal(barrier, inc=1, device_id=dev, device_id_type=MESH)

    l_j.wait()
    for c in range(C):
        part = jin[...].astype(F32)[:, c * tc:(c + 1) * tc, :]
        jb[c, t] = part.reshape(npair * tc, kslice).astype(BF)

    pl.semaphore_wait(barrier, len(peers))

    xl, xr, x2 = mod(x - 1, 4), mod(x + 1, 4), mod(x + 2, 4)
    sl, sr, s2 = xl * 2 + core, xr * 2 + core, x2 * 2 + core
    sib = at(cc=1 - core)

    def xsend(name, c, slot, dev):
        remote(f"{name}{c}", jb.at[c, slot], jb.at[c, slot], dev, f"x{c}", jb.at[c, pl.ds(0, 7)])

    def X0(c):
        xsend("x2", c, t, at(xx=x2))
        xsend("xl", c, t, at(xx=xr))
        xsend("xr", c, t, at(xx=xl))
        xsend("sb", c, t, sib)

    def XF(c):
        for name, slot in (("xl", sl), ("xr", sr), ("x2", s2)):
            arrived(f"{name}{c}", jb.at[c, slot])
            xsend("sb", c, slot, sib)

    def piece(c, i):
        return jnp.dot(jb[c, i], wq_v[pl.ds(pl.multiple_of(i * kslice, kslice), kslice), :],
                       preferred_element_type=F32)

    def Q(c):
        q = piece(c, t) + piece(c, sl) + piece(c, sr) + piece(c, s2)
        arrived(f"sb{c}", jb.at[c, pl.ds(0, 4)])
        for slot in (t, sl, sr, s2):
            q = q + piece(c, slot + 1 - 2 * core)
        heads = [q[:, h * HD:(h + 1) * HD].reshape(npair, tc, HD) for h in range(4)]
        qb[c][...] = jnp.concatenate(heads, 1).astype(BF)

    def MZ():
        for n in (1, 2, 3):
            remote("mz", mt.at[y, 0], mt.at[y, n], at(zz=zt[n]), "mz", mt.at[y, pl.ds(0, 3)])
        remote("len", lt.at[odd], lt.at[odd], at(zz=z + 1 - 2 * odd), "len", lt.at[odd])

    late = []

    def MY():
        arrived("mz", mt.at[y, pl.ds(1, 3)])
        for d in (1, 2, 3):
            remote("my", mt.at[y], mt.at[y], at(yy=mod(y + d, 4)), "my", mt.at[pl.ds(0, 3)])
        late.append(local(mt.at[y], smr))

    def ML():
        arrived("my", mt.at[pl.ds(0, 3)])
        arrived("len", lt.at[1 - odd])
        late.append(local(mt, sm))
        late.append(local(lt, ls))

    def MR():
        late[0].wait()

    def MW():
        late[1].wait()
        late[2].wait()

    def masked(v, length):
        keys = lax.broadcasted_iota(I32, (v.shape[0], 2 * HD), 0)
        both = jnp.concatenate([v.astype(F32), jnp.ones(v.shape, F32)], 1)
        return jnp.where(keys < length, both, 0.0).astype(BF)

    def KV(r):
        if r == 0:
            l_kv.wait()
        l_h[r].wait()
        kv = jnp.dot(hid_v[r], wkv_v[...], preferred_element_type=F32).astype(BF)
        kvx[odd, r, 0] = kv[:, :HD]
        kvx[odd, r, 1] = kv[:, HD:]
        vext[odd, r] = masked(kv[:, HD:], lens[r])
        remote("kv", kvx.at[odd, r], kvx.at[odd, r], at(zz=z + 1 - 2 * odd),
               "kv", kvx.at[odd])

    def VP():
        other = 1 - odd
        arrived("kv", kvx.at[other])

        def one(r, carry):
            vext[other, r] = masked(kvx[other, r, 1], ls[other, 0, r])
            return carry

        lax.fori_loop(0, 4, one, 0)

    def QP(r):
        q = jnp.dot(hid_v[r], wq_v[...], preferred_element_type=F32).astype(BF)
        for h in range(4):
            qself[r, h] = q[:, h * HD:(h + 1) * HD]

    enc_out = []

    def SA(r):
        k_r = kvx[odd, r, 0]
        v_r = vext[odd, r]
        for h in range(4):
            for b in range(2):
                n = (b + 1) * 128
                s = lax.dot_general(qself[r, h, b * 128:(b + 1) * 128, :], k_r[:n],
                                    (((1,), (1,)), ((), ())), preferred_element_type=F32)
                qi = lax.broadcasted_iota(I32, (128, n), 0) + b * 128
                ti = lax.broadcasted_iota(I32, (128, n), 1)
                w = jnp.where(ti <= qi, weights_of(s), 0.0).astype(BF)
                ne = jnp.dot(w, v_r[:n], preferred_element_type=F32)
                oenc[r, b * 128:(b + 1) * 128, h * HD:(h + 1) * HD] = (
                    ne[:, :HD] / ne[:, HD:]).astype(BF)
        enc_out.append(local(oenc.at[r], enc.at[r]))

    def Z(c):
        for n in (3, 2, 1, 0):
            for k in range(8):
                block = qb[c][jnp.bitwise_and(sm0[4, n * 8 + k], npair - 1)]
                if n:
                    zs[c, n - 1, k] = block
                else:
                    zq[c][0][k] = block
            if n:
                remote(f"z{c}{n}", zs.at[c, n - 1], zq[c][n], at(zz=zt[n]), f"z{c}", zs.at[c])

    def Y(c, n):
        if n:
            arrived(f"z{c}{n}", zq[c][n])
        tile = smr.at[n] if n else sm0
        for d in (2, 1, 3, 0):
            yy = mod(y + d, 4)
            for s in range(4):
                which = jnp.bitwise_and(tile[s % 2, (2 * band + s // 2) * 4 + yy], 7)
                block = zq[c][n][which]
                if d:
                    ys[c, n, d - 1, s] = block
                else:
                    yq[c, n, y, s] = block
            if d:
                remote(f"y{c}{n}", ys.at[c, n, d - 1], yq.at[c, n, y], at(yy=yy), f"y{c}", ys.at[c])

    diag = lax.broadcasted_iota(I32, (rows, 128), 0) == lax.broadcasted_iota(I32, (rows, 128), 1)
    sub16 = lax.broadcasted_iota(I32, (16, 128), 0)

    def A(c, n):
        arrived(f"y{c}{n}", yq.at[c, n, pl.ds(0, 3)])

        def one(src, carry):
            dens = []
            for s in range(4):
                zz, j = s // 2, s % 2
                it = jnp.bitwise_and(sm[src, n, 2 + j, (2 * band + zz) * 4 + y], 3)
                sc = lax.dot_general(yq[c, n, src, s], kvx[zz, it, 0],
                                     (((1,), (1,)), ((), ())), preferred_element_type=F32)
                ne = jnp.dot(weights_of(sc).astype(BF), vext[zz, it], preferred_element_type=F32)
                rs[c, n, src, s * per:(s + 1) * per] = ne[:, :HD].astype(BF).reshape(per, 16, HD)
                dens.append(jnp.sum(jnp.where(diag, ne[:, HD:], 0.0), 0, keepdims=True))
            den = jnp.concatenate(dens, 0)
            high = den.astype(BF).astype(F32)
            rs[c, n, src, 4 * per] = jnp.concatenate(
                [high, den - high, jnp.zeros((8, 128), F32)], 0).astype(BF)
            return carry

        lax.fori_loop(0, 4, one, 0, unroll=4)
        for d in (2, 1, 3):
            yy = mod(y + d, 4)
            remote(f"r{c}{n}", rs.at[c, n, yy], yr[c][n].at[y], at(yy=yy), f"r{c}", rs.at[c, pl.ds(0, 3)])
        yr[c][n][y] = rs[c, n, y]

    def R(c, n):
        arrived(f"r{c}{n}", yr[c][n].at[pl.ds(0, 3)])
        tile = smr.at[n] if n else sm0
        for k in range(8):
            num, den = [], []
            for side in (0, 1):
                p = jnp.bitwise_and(tile[5 + side, n * 8 + k], 15)
                src, s = p // 4, lax.rem(p, 4)
                num.append(yr[c][n][src, pl.ds(s * per, per)].reshape(rows, HD).astype(F32))
                dens = yr[c][n][src, 4 * per].astype(F32)
                den.append(jnp.where((sub16 == s) | (sub16 == s + 4), dens, 0.0))
            total = jnp.sum(den[0] + den[1], 0, keepdims=True)
            total = jnp.sum(jnp.where(diag, total, 0.0), 1, keepdims=True)
            block = ((num[0] + num[1]) / total).astype(BF)
            if n:
                zr[c, n - 1, k] = block
            else:
                hret[c][k] = block
        if n:
            remote(f"h{c}", zr.at[c, n - 1], hret[c].at[pl.ds(n * 8, 8)], at(zz=zh[n]), f"h{c}", zr.at[c])

    def H():
        for c in range(C):
            arrived(f"h{c}", hret[c].at[pl.ds(8, 24)])
        for p in range(npair):
            spot_p = jnp.bitwise_and(sm0[7, p], 31)
            got = [hret[c][spot_p].astype(F32) for c in range(C)]
            for h in range(4):
                opair[p, :, h * HD:(h + 1) * HD] = jnp.concatenate(
                    [g[h * tc:(h + 1) * tc] for g in got], 0).astype(BF)
        enc_out.append(local(opair, pair))

    for c in range(C):
        X0(c)

    lane = lax.broadcasted_iota(I32, (npair, 128), 1)
    sub = lax.broadcasted_iota(I32, (npair, 128), 0)
    eye = lax.broadcasted_iota(I32, (npair, npair), 0) == lax.broadcasted_iota(I32, (npair, npair), 1)

    def column(row):
        return jnp.sum(jnp.where(eye, row, 0), 1, keepdims=True)

    dev0, dev1, item = column(pdev[0:1, :]), column(pdev[1:2, :]), column(pitem[0:1, :])
    strict = jnp.where(
        lax.broadcasted_iota(I32, (npair, npair), 1) < lax.broadcasted_iota(I32, (npair, npair), 0),
        1.0, 0.0).astype(F32)
    m0 = jnp.where(dev0 == lane, 1.0, 0.0)
    m1 = jnp.where(dev1 == lane, 1.0, 0.0)
    m = m0 + m1
    rank = jnp.dot(strict, m, preferred_element_type=F32)
    rel = jnp.bitwise_and(lax.shift_right_logical(dev0, 3) - band + 4, 3)
    near = jnp.where(rel == 0, 0, jnp.where(rel == 2, 3, jnp.where((rel == 1) == (odd == 1), 1, 2)))
    mb = jnp.where(near == lane, 1.0, 0.0)
    place = jnp.sum(mb * jnp.dot(strict, mb, preferred_element_type=F32), 1, keepdims=True)
    home = near.astype(F32) * 8.0 + place
    at_home = jnp.where(home == lane.astype(F32), 1.0, 0.0)

    def down(v):
        return jnp.sum(v, 0, keepdims=True)

    first = jnp.where(rank == 0.0, m, 0.0)
    second = jnp.where(rank == 1.0, m, 0.0)
    spot = (jnp.bitwise_and(lane, 3) * 4
            + jnp.bitwise_and(lax.shift_right_logical(lane, 2), 1) * 2).astype(F32) + rank
    pos0 = jnp.sum(m0 * spot, 1, keepdims=True)
    pos1 = jnp.sum(m1 * spot, 1, keepdims=True)
    itemf = item.astype(F32)
    subf = sub.astype(F32)
    table = jnp.concatenate([
        down(first * place), down(second * place), down(first * itemf), down(second * itemf),
        down(at_home * subf), down(at_home * pos0), down(at_home * pos1),
        down(jnp.where(sub == lane, home, 0.0))], 0)
    mt[y, 0] = table.astype(I32)
    l_0 = local(mt.at[y, 0], sm0)
    lane8 = lax.broadcasted_iota(I32, (8, 128), 1)
    lt[odd] = jnp.where(lane8 == 0, lens[0], jnp.where(lane8 == 1, lens[1],
                        jnp.where(lane8 == 2, lens[2], lens[3])))

    MZ()
    stages = {"XF": XF, "MR": MR, "MW": MW, "Q": Q, "KV": KV, "QP": QP, "SA": SA, "Z": Z, "Y": Y, "A": A,
              "R": R, "MY": MY, "ML": ML, "VP": VP, "H": H}
    waited = []
    for word in SCHED:
        name = word.rstrip("0123456789")
        if name in ("Q", "QP") and not waited:
            l_q.wait()
            l_0.wait()
            waited.append(word)
        stages[name](*[int(d) for d in word[len(name):]])
    for copy in enc_out:
        copy.wait()
    for slot, total in finals:
        pltpu.make_async_remote_copy(
            src_ref=total, dst_ref=total, send_sem=ssem.at[slot], recv_sem=rsem.at[0],
            device_id=(dp, t), device_id_type=MESH).wait_send()


def copy_kernel(enc, pair, enc_out, pair_out, enc_v, pair_v, sem):
    steps = [(enc.at[r], enc_v.at[r], enc_out.at[r]) for r in range(4)] + [(pair, pair_v, pair_out)]
    inward = [pltpu.make_async_copy(src, mid, sem.at[k]) for k, (src, mid, _) in enumerate(steps)]
    outward = [pltpu.make_async_copy(mid, dst, sem.at[5 + k]) for k, (_, mid, dst) in enumerate(steps)]
    for copy in inward:
        copy.start()
    for first, second in zip(inward, outward):
        first.wait()
        second.start()
    for copy in outward:
        copy.wait()


def copied(encoded, attended):
    spec = pl.BlockSpec(memory_space=pl.ANY)
    return pl.pallas_call(
        copy_kernel,
        out_shape=[jax.ShapeDtypeStruct(a.shape, a.dtype) for a in (encoded, attended)],
        in_specs=[spec, spec], out_specs=[spec, spec],
        scratch_shapes=[pltpu.VMEM(encoded.shape, BF), pltpu.VMEM(attended.shape, BF),
                        pltpu.SemaphoreType.DMA((10,))],
        name="results",
    )(encoded, attended)


def on_device(hidden, lengths, judge, w_query, w_keyval, pair_devices, pair_items):
    npair, ntok, kslice = judge.shape
    nresp, seq, width = hidden.shape
    rows = ntok // C * 4
    V = pltpu.VMEM
    scratch = [
        V((nresp, seq, width), BF), V(w_query.shape, BF), V(w_keyval.shape, BF), V(judge.shape, BF),
        V((C, 8, npair * ntok // C, kslice), BF), V((nresp, 4, seq, HD), BF),
        V((2, 4, 2, seq, HD), BF), V((2, 4, seq, 2 * HD), BF),
        V((C, 3, 8, rows, HD), BF), V((C, 4, 3, 4, rows, HD), BF), V((C, 4, 4, 4, rows, HD), BF),
        V((C, 4, 4, rows // 4 + 1, 16, HD), BF), V((C, 3, 8, rows, HD), BF),
        V((4, 4, 8, 128), I32), pltpu.SMEM((4, 4, 8, 128), I32), pltpu.SMEM((4, 8, 128), I32), pltpu.SMEM((8, 128), I32),
        V((2, 8, 128), I32), pltpu.SMEM((2, 8, 128), I32),
        V((nresp, seq, 4 * HD), BF), V((npair, ntok, 4 * HD), BF),
        pltpu.SemaphoreType.DMA((16,)), pltpu.SemaphoreType.DMA((5 * C + 4,)), pltpu.SemaphoreType.DMA((16 * C + 4,)),
        [V((npair, rows, HD), BF) for _ in range(C)],
        [[V((8, rows, HD), BF) for _ in range(4)] for _ in range(C)],
        [[V((4, rows // 4 + 1, 16, HD), BF) for _ in range(4)] for _ in range(C)],
        [V((32, rows, HD), BF) for _ in range(C)],
    ]
    flat, tree = jax.tree.flatten(scratch, is_leaf=lambda s: not isinstance(s, list))

    def body(*refs):
        nested = jax.tree.unflatten(tree, refs[9:])
        kernel(*refs[:9], *nested)

    any_, vm, sm = pl.BlockSpec(memory_space=pl.ANY), pl.BlockSpec(memory_space=V), pl.BlockSpec(memory_space=pltpu.SMEM)
    encoded, attended = pl.pallas_call(
        body,
        out_shape=[jax.ShapeDtypeStruct((nresp, seq, 4 * HD), BF),
                   jax.ShapeDtypeStruct((npair, ntok, 4 * HD), BF)],
        in_specs=[any_, any_, any_, any_, sm, vm, vm],
        out_specs=[any_, any_],
        scratch_shapes=flat,
        compiler_params=pltpu.CompilerParams(
            collective_id=0, has_side_effects=True, vmem_limit_bytes=56 * 2 ** 20),
        name="judge",
    )(judge, hidden, w_query, w_keyval, lengths, pair_devices.T, pair_items.T)
    return copied(encoded, attended)


def solution(mesh):
    return jax.shard_map(
        on_device,
        mesh=mesh,
        in_specs=(
            P("dp", None, None),
            P("dp"),
            P("dp", None, "tensor"),
            P(None, "tensor"),
            P(None, "tensor"),
            P("dp", None),
            P("dp", None),
        ),
        out_specs=(P("dp", None, "tensor"), P("dp", None, "tensor")),
        check_vma=False,
    )
```

time: 316 us -> 62.2 us (0.20)
  the two profiles are of different devices: /device:TPU:28 before, /device:TPU:32 now
where the time goes in v1:
time: 62.2 us; the launch traced here: 62.1 us
  Pallas kernels  61.3 us (99%)
  between operations  0.8 us (1%)
    pallas_call x1, Pallas kernels, on_device(): pl.pallas_call(body, out_shape=[jax.ShapeDtypeStruct((nresp, seq, 4 * HD)...  59.2 us
    pallas_call x1, Pallas kernels, copied(): pl.pallas_call(copy_kernel, out_shape=[jax.ShapeDtypeStruct(a.shape, a.dt...  2.08 us

profile of v1, /device:TPU:32, one launch (start us, length us, event | category | flops | bytes accessed | tf_op | source)
XLA Modules:
  0.0 62.1 jit_solution(4462342180515457698)
XLA Ops:
  0.6 59.2 %judge.1 = (bf16[4,256,512]{2,1,0:T(8,128)(2,1)}, bf16[16,16,512]{2,1,0:T(8,128)(2,1)}) custom-call(bf16[16,16,512]{2,1,0:T(8,128)(2,1)} %refs_0_.1, bf16[4,256,4096]{2,1,0:T(8,128)(2,1)} %refs_1_.1, bf16[4096,512]{1,0:T(8,128)(2,1)} %refs_2_.1, bf16[4096,256]{1,0:T(8,128)(2,1)} %refs_3_.1, s32[4]{0:T(128)} %refs_4_.1, s32[2,16]{1,0:T(2,128)} %bitcast.2, ...), custom_call_target="tpu_custom_call" | custom-call | tf_op jit(solution)/shard_map/judge/pallas_call | solution.py:416
  59.8 2.1 %results.1 = (bf16[4,256,512]{2,1,0:T(8,128)(2,1)}, bf16[16,16,512]{2,1,0:T(8,128)(2,1)}) custom-call(bf16[4,256,512]{2,1,0:T(8,128)(2,1)} %get-tuple-element.4.enc, bf16[16,16,512]{2,1,0:T(8,128)(2,1)} %get-tuple-element.5.pair), custom_call_target="tpu_custom_call" | custom-call | tf_op jit(solution)/shard_map/results/pallas_call | solution.py:379

commit v2 on v1

--- a/solution.py
+++ b/solution.py
@@ -19,12 +19,12 @@
 SCHED = (
     "KV0", "KV1", "KV2", "KV3", "XF0", "MY", "Q0", "MR", "Z0", "QP0",
     "XF1", "Y00", "Q1", "Z1", "QP1", "ML", "Y10", "XF2", "Q2", "MW",
-    "Z2", "QP2", "Y20", "XF3", "Q3", "Z3", "QP3", "Y30", "VP", "A00",
-    "Y03", "Y02", "Y01", "A10", "R00", "A20", "Y13", "Y12", "Y11", "A30",
-    "A03", "Y23", "Y22", "Y21", "A02", "R10", "R20", "Y33", "A01", "Y32",
-    "Y31", "A13", "R30", "A12", "R03", "A11", "SA0", "A23", "A22", "R02",
-    "A21", "R01", "A33", "A32", "R13", "R12", "A31", "SA1", "R11", "R23",
-    "R22", "SA2", "R21", "R33", "R32", "SA3", "R31", "H",
+    "Z2", "Y20", "XF3", "Q3", "Z3", "Y30", "QP2", "VP", "A00", "Y03",
+    "Y02", "Y01", "A10", "A20", "Y13", "Y12", "Y11", "A03", "A30", "Y23",
+    "Y22", "Y21", "A02", "A01", "Y33", "Y32", "Y31", "R00", "R10", "A13",
+    "A12", "R20", "R30", "R03", "A11", "A23", "R02", "A22", "R01", "A21",
+    "A33", "R13", "A32", "R12", "A31", "QP3", "R11", "R23", "R22", "R21",
+    "SA0", "SA1", "R33", "R32", "R31", "SA2", "SA3", "H",
 )
 
 
@@ -86,9 +86,8 @@
 
     l_j = local(judge, jin)
     l_kv = local(wkv, wkv_v)
-    l_h = [local(hidden.at[0], hid_v.at[0]), local(hidden.at[1], hid_v.at[1])]
+    l_h = [local(hidden.at[r], hid_v.at[r]) for r in range(4)]
     l_q = local(wq, wq_v)
-    l_h += [local(hidden.at[2], hid_v.at[2]), local(hidden.at[3], hid_v.at[3])]
 
     barrier = pltpu.get_barrier_semaphore()
     peers = [at(xx=mod(x + d, 4)) for d in (1, 2, 3)] + [at(cc=1 - core)]
@@ -98,10 +97,11 @@
         pl.semaphore_signal(barrier, inc=1, device_id=dev, device_id_type=MESH)
 
     l_j.wait()
-    for c in range(C):
+    def cut(c):
         part = jin[...].astype(F32)[:, c * tc:(c + 1) * tc, :]
         jb[c, t] = part.reshape(npair * tc, kslice).astype(BF)
 
+    cut(0)
     pl.semaphore_wait(barrier, len(peers))
 
     xl, xr, x2 = mod(x - 1, 4), mod(x + 1, 4), mod(x + 2, 4)
@@ -297,6 +297,8 @@
         enc_out.append(local(opair, pair))
 
     for c in range(C):
+        if c:
+            cut(c)
         X0(c)
 
     lane = lax.broadcasted_iota(I32, (npair, 128), 1)

time: 62.2 us -> 61.4 us (0.987)
  Pallas kernels: 61.3 us -> 60.5 us
    pallas_call x1, Pallas kernels: 59.2 us -> 58.4 us  [on_device(): pl.pallas_call(body, out_shape=[jax.ShapeDtypeStruct((nresp, seq, 4 * HD)...]
where the time goes in v2:
time: 61.4 us; the launch traced here: 61.3 us
  Pallas kernels  60.5 us (99%)
  between operations  0.8 us (1%)
    pallas_call x1, Pallas kernels, on_device(): pl.pallas_call(body, out_shape=[jax.ShapeDtypeStruct((nresp, seq, 4 * HD)...  58.4 us
    pallas_call x1, Pallas kernels, copied(): pl.pallas_call(copy_kernel, out_shape=[jax.ShapeDtypeStruct(a.shape, a.dt...  2.08 us

profile of v2, /device:TPU:32, one launch (start us, length us, event | category | flops | bytes accessed | tf_op | source)
XLA Modules:
  0.0 61.3 jit_solution(6589961950952916956)
XLA Ops:
  0.6 58.4 %judge.1 = (bf16[4,256,512]{2,1,0:T(8,128)(2,1)}, bf16[16,16,512]{2,1,0:T(8,128)(2,1)}) custom-call(bf16[16,16,512]{2,1,0:T(8,128)(2,1)} %refs_0_.1, bf16[4,256,4096]{2,1,0:T(8,128)(2,1)} %refs_1_.1, bf16[4096,512]{1,0:T(8,128)(2,1)} %refs_2_.1, bf16[4096,256]{1,0:T(8,128)(2,1)} %refs_3_.1, s32[4]{0:T(128)} %refs_4_.1, s32[2,16]{1,0:T(2,128)} %bitcast.2, ...), custom_call_target="tpu_custom_call" | custom-call | tf_op jit(solution)/shard_map/judge/pallas_call | solution.py:418
  59.0 2.1 %results.1 = (bf16[4,256,512]{2,1,0:T(8,128)(2,1)}, bf16[16,16,512]{2,1,0:T(8,128)(2,1)}) custom-call(bf16[4,256,512]{2,1,0:T(8,128)(2,1)} %get-tuple-element.4.enc, bf16[16,16,512]{2,1,0:T(8,128)(2,1)} %get-tuple-element.5.pair), custom_call_target="tpu_custom_call" | custom-call | tf_op jit(solution)/shard_map/results/pallas_call | solution.py:381

commit v3 on v2

--- a/solution.py
+++ b/solution.py
@@ -23,8 +23,8 @@
     "Y02", "Y01", "A10", "A20", "Y13", "Y12", "Y11", "A03", "A30", "Y23",
     "Y22", "Y21", "A02", "A01", "Y33", "Y32", "Y31", "R00", "R10", "A13",
     "A12", "R20", "R30", "R03", "A11", "A23", "R02", "A22", "R01", "A21",
-    "A33", "R13", "A32", "R12", "A31", "QP3", "R11", "R23", "R22", "R21",
-    "SA0", "SA1", "R33", "R32", "R31", "SA2", "SA3", "H",
+    "A33", "R13", "A32", "R12", "A31", "R11", "R23", "R22", "R21", "SA0",
+    "SA1", "R33", "R32", "R31", "QP3", "SA2", "SA3", "H",
 )
 
 

time: 61.4 us -> 61.8 us (level); the launches traced: 61.3 us -> 60.8 us
  no operation moved by 1% of the time
where the time goes in v3:
time: 61.8 us; the launch traced here: 60.8 us
  Pallas kernels  60 us (97%)
  between operations  0.8 us (1%)
    pallas_call x1, Pallas kernels, on_device(): pl.pallas_call(body, out_shape=[jax.ShapeDtypeStruct((nresp, seq, 4 * HD)...  57.9 us
    pallas_call x1, Pallas kernels, copied(): pl.pallas_call(copy_kernel, out_shape=[jax.ShapeDtypeStruct(a.shape, a.dt...  2.08 us

profile of v3, /device:TPU:32, one launch (start us, length us, event | category | flops | bytes accessed | tf_op | source)
XLA Modules:
  0.0 60.8 jit_solution(3279891768596914563)
XLA Ops:
  0.6 57.9 %judge.1 = (bf16[4,256,512]{2,1,0:T(8,128)(2,1)}, bf16[16,16,512]{2,1,0:T(8,128)(2,1)}) custom-call(bf16[16,16,512]{2,1,0:T(8,128)(2,1)} %refs_0_.1, bf16[4,256,4096]{2,1,0:T(8,128)(2,1)} %refs_1_.1, bf16[4096,512]{1,0:T(8,128)(2,1)} %refs_2_.1, bf16[4096,256]{1,0:T(8,128)(2,1)} %refs_3_.1, s32[4]{0:T(128)} %refs_4_.1, s32[2,16]{1,0:T(2,128)} %bitcast.2, ...), custom_call_target="tpu_custom_call" | custom-call | tf_op jit(solution)/shard_map/judge/pallas_call | solution.py:418
  58.6 2.1 %results.1 = (bf16[4,256,512]{2,1,0:T(8,128)(2,1)}, bf16[16,16,512]{2,1,0:T(8,128)(2,1)}) custom-call(bf16[4,256,512]{2,1,0:T(8,128)(2,1)} %get-tuple-element.4.enc, bf16[16,16,512]{2,1,0:T(8,128)(2,1)} %get-tuple-element.5.pair), custom_call_target="tpu_custom_call" | custom-call | tf_op jit(solution)/shard_map/results/pallas_call | solution.py:381
